TPU v7x, 512 devices: a whole 4x4x16 slice. The times are simulated.
512 devices in a mesh: tm: 64 (over z, x_hi, core), mic: 8 (over x_lo, y).
Axes of the slice: x: 4 (x_hi: 2, x_lo: 2; x = x_hi * 2 + x_lo), y: 4, z: 16, core: 2. Of those that a mesh axis runs over, the one named last changes fastest.
Arguments:
- signal: bfloat16 [262144, 4096], P('tm', 'mic')
- mic_pos: int32 [3, 4096], P(None, 'mic'), may hold values from 0 to 255, as said below
- grid_pos: int32 [3, 8192], replicated, may hold values from 0 to 255, as said below
- bins: int32 [2], replicated, may hold values from 1 to 511, as said below
Outputs:
- power: float32 [8192], P('mic')
Inputs may be any that keep to these rules, and one draw needn't show every extreme that they name: `mic_pos`: rows are x, y, z; a microphone's z is below 16. `grid_pos`: rows are x, y, z; a grid point's z is 64 or more and below 128. `bins`: the bin indices are distinct; the first is 511.
All inputs are finite; a program needn't handle non-finite values.
Results may differ from a plain program's by a relative error of at most 0.0006.
The roundings to bfloat16 on the way count: a program that leaves them out, or rounds other values in their place, can miss the bound.
Values may be sent and summed in bfloat16 or wider, within the bound.
A program may use at most 64 MiB of HBM per device.

v0:
```python
import math
import jax
import jax.numpy as jnp
from jax import lax
from jax.sharding import PartitionSpec as P

MICS = 4096
SEGLEN = 8192
NBINS = 2


def from_behind(shard, axis, by):
    size = lax.axis_size(axis)
    pairs = [(i, i + by) for i in range(size) if 0 <= i + by < size]
    return lax.ppermute(shard, axis, pairs)


def fourier_rows(bins):
    sample_index = jnp.arange(SEGLEN, dtype=jnp.int32)
    window = 0.5 - 0.5 * jnp.cos(2.0 * math.pi * sample_index.astype(jnp.float32) / SEGLEN)
    phases = bins[:, None] * sample_index[None, :] % SEGLEN
    angles = 2.0 * math.pi * phases.astype(jnp.float32) / SEGLEN
    weighting = window / math.sqrt(0.375 * SEGLEN)
    fourier = jnp.stack([weighting * jnp.cos(angles), -weighting * jnp.sin(angles)], axis=1)
    return fourier.reshape(2 * NBINS, SEGLEN).astype(jnp.bfloat16)


def steer_block(points, mic_pos, bins):
    offsets = points[:, :, None] - mic_pos[:, None, :]
    distance = jnp.sqrt(jnp.sum(offsets * offsets, axis=0).astype(jnp.float32))
    strength = 16.0 / distance
    cycles = bins.astype(jnp.float32)[:, None, None] * distance[None] * (16.0 / SEGLEN)
    cosine_part = (strength[None] * jnp.cos(2.0 * math.pi * cycles)).astype(jnp.bfloat16)
    sine_part = (strength[None] * jnp.sin(2.0 * math.pi * cycles)).astype(jnp.bfloat16)
    return (cosine_part, sine_part)


def steered(spectra, cosine_part, sine_part):
    segments = spectra.shape[0]
    mic_count = spectra.shape[2]
    width = cosine_part.shape[1]
    per_bin = []
    for bin_index in range(NBINS):
        bin_pair = spectra[:, 2 * bin_index : 2 * bin_index + 2, :].reshape(2 * segments, mic_count)
        cosine_sum = jnp.dot(
            bin_pair, cosine_part[bin_index].T, preferred_element_type=jnp.float32
        ).reshape(segments, 2, width)
        sine_sum = jnp.dot(
            bin_pair, sine_part[bin_index].T, preferred_element_type=jnp.float32
        ).reshape(segments, 2, width)
        real_part = cosine_sum[:, 0] - sine_sum[:, 1]
        imag_part = cosine_sum[:, 1] + sine_sum[:, 0]
        per_bin.append(jnp.stack([real_part, imag_part], axis=1))
    return jnp.stack(per_bin, axis=1)


def beams_for(spectra, chosen_points, mic_pos, bins):
    point_count = chosen_points.shape[1]
    block_width = min(point_count, 1024)
    block_count = point_count // block_width
    points = chosen_points.reshape(3, block_count, block_width).transpose(1, 0, 2)

    def block_beam(block_points):
        cosine_part, sine_part = steer_block(block_points, mic_pos, bins)
        return steered(spectra, cosine_part, sine_part)

    partial_value = lax.map(block_beam, points)
    segments = spectra.shape[0]
    return partial_value.transpose(1, 2, 3, 0, 4).reshape(segments, NBINS, 2, point_count)


def local(signal, mic_pos, grid_pos, bins):
    fourier = fourier_rows(bins)
    following = from_behind(signal, "tm", -1)
    segment = jnp.concatenate([signal, following], axis=0)
    spectrum = jnp.dot(fourier, segment, preferred_element_type=jnp.float32)
    spectrum = spectrum.astype(jnp.bfloat16)
    grid_count = grid_pos.shape[1]
    owners = lax.axis_size("mic")
    owned_count = grid_count // owners
    spans = lax.axis_size("tm")
    partial_value = beams_for(spectrum[None], grid_pos, mic_pos, bins)[0]
    summed = lax.psum(partial_value, "mic")
    owned = lax.dynamic_slice_in_dim(summed, lax.axis_index("mic") * owned_count, owned_count, 2)
    local_power = jnp.sum(owned * owned, axis=(0, 1))
    power_sum = lax.psum(local_power, "tm")
    return power_sum / (spans * NBINS * MICS)


def solution(mesh):
    in_specs = (P("tm", "mic"), P(None, "mic"), P(), P())
    out_specs = P("mic")
    return jax.shard_map(local, mesh=mesh, in_specs=in_specs, out_specs=out_specs, check_vma=False)
```

profile of v0, /device:TPU:1, one launch (start us, length us, event | category | flops | bytes accessed | tf_op | source)
XLA Modules:
  0.0 457.2 jit_solution(10412396298532731741)
XLA Ops:
  6.5 8.8 %collective-permute-start = (bf16[4096,512]{1,0:T(8,128)(2,1)}, bf16[4096,512]{1,0:T(8,128)(2,1)}, u32[]{:S(2)}, u32[]{:S(2)}) collective-permute-start(bf16[4096,512]{1,0:T(8,128)(2,1)} %param.6), channel_id=1, source_target_pairs={{8,0},{16,8},{24,16},{32,24},{40,32},{48,40},{56,48},{64,56},{72,6... | collective-permute-start | bytes 12582920 | tf_op jit(solution)/shard_map/ppermute | solution.py:15
  15.5 1.9 multiply_convert_fusion.3
  17.6 0.7 convert_bitcast_fusion
  18.3 40.8 %collective-permute-done = bf16[4096,512]{1,0:T(8,128)(2,1)} collective-permute-done((bf16[4096,512]{1,0:T(8,128)(2,1)}, bf16[4096,512]{1,0:T(8,128)(2,1)}, u32[]{:S(2)}, u32[]{:S(2)}) %collective-permute-start) | collective-permute-done | bytes 4194336 | tf_op jit(solution)/shard_map/ppermute | solution.py:15
  59.1 4.6 %fusion.16 = bf16[1,4,512]{2,1,0:T(4,128)(2,1)S(1)} fusion(bf16[4,8192]{1,0:T(4,128)(2,1)S(1)} %convert_element_type.74, bf16[4096,512]{1,0:T(8,128)(2,1)} %collective-permute-done, bf16[4096,512]{1,0:T(8,128)(2,1)} %param.6), kind=kOutput, calls=%fused_computation.36 | convolution fusion | flops 50333696 | bytes 8458240 | tf_op jit(solution)/shard_map/dot_general | solution.py:76
  63.7 161.1 %while.12 = (s32[]{:T(128)}, f32[8,1,2,2,1024]{4,3,2,1,0:T(2,128)S(1)}, s32[8,3,1024]{2,1,0:T(4,128)}, s32[3,512]{1,0:T(4,128)S(1)}, f32[2,1,1]{0,2,1:T(1,128)S(1)}, /*index=5*/bf16[1,4,512]{2,1,0:T(4,128)(2,1)S(1)}, s32[]{:T(128)}) while((s32[]{:T(128)}, f32[8,1,2,2,1024]{4,3,2,1,0:T(2,128)S(1)}, s32[8,3,1024]{2,1,0:T(4,128)}, ...), condition=%wide.region_2.3_spmd, body=%wide.region_0.2_spmd.sunk | while | flops 19935232 | bytes 21170268 | solution.py:67
  63.7 0.7 dynamic-slice_bitcast_fusion.2
  64.5 0.9 multiply_reduce_fusion.3
  65.4 0.7 rsqrt_multiply_fusion.2
  66.1 16.1 %multiply_convert_fusion.5 = (bf16[2,1024,512]{2,1,0:T(8,128)(2,1)S(1)}, bf16[2,1024,512]{2,1,0:T(8,128)(2,1)S(1)}) fusion(f32[1024,512]{1,0:T(8,128)S(1)} %get-tuple-element.158, f32[2]{0:T(128)S(1)} %bitcast.94, f32[1024,512]{1,0:T(8,128)S(1)} %get-tuple-element.159), kind=kLoop, calls=%fused_computation.2.clone.1 | loop fusion | flops 6291456 | bytes 8388616 | tf_op jit(solution)/shard_map/while/body/eval_jaxpr/convert_element_type | solution.py:33
  83.9 0.7 dynamic-slice_bitcast_fusion.2
  84.6 0.9 multiply_reduce_fusion.3
  85.5 0.7 rsqrt_multiply_fusion.2
  86.2 16.1 %multiply_convert_fusion.5 = (bf16[2,1024,512]{2,1,0:T(8,128)(2,1)S(1)}, bf16[2,1024,512]{2,1,0:T(8,128)(2,1)S(1)}) fusion(f32[1024,512]{1,0:T(8,128)S(1)} %get-tuple-element.158, f32[2]{0:T(128)S(1)} %bitcast.94, f32[1024,512]{1,0:T(8,128)S(1)} %get-tuple-element.159), kind=kLoop, calls=%fused_computation.2.clone.1 | loop fusion | flops 6291456 | bytes 8388616 | tf_op jit(solution)/shard_map/while/body/eval_jaxpr/convert_element_type | solution.py:33
  102.7 0.4 convolution_bitcast_fusion.11
  104.0 0.7 dynamic-slice_bitcast_fusion.2
  104.7 0.9 multiply_reduce_fusion.3
  105.7 0.7 rsqrt_multiply_fusion.2
  106.4 16.1 %multiply_convert_fusion.5 = (bf16[2,1024,512]{2,1,0:T(8,128)(2,1)S(1)}, bf16[2,1024,512]{2,1,0:T(8,128)(2,1)S(1)}) fusion(f32[1024,512]{1,0:T(8,128)S(1)} %get-tuple-element.158, f32[2]{0:T(128)S(1)} %bitcast.94, f32[1024,512]{1,0:T(8,128)S(1)} %get-tuple-element.159), kind=kLoop, calls=%fused_computation.2.clone.1 | loop fusion | flops 6291456 | bytes 8388616 | tf_op jit(solution)/shard_map/while/body/eval_jaxpr/convert_element_type | solution.py:33
  122.9 0.4 convolution_bitcast_fusion.11
  124.1 0.7 dynamic-slice_bitcast_fusion.2
  124.9 0.9 multiply_reduce_fusion.3
  125.8 0.7 rsqrt_multiply_fusion.2
  126.5 16.1 %multiply_convert_fusion.5 = (bf16[2,1024,512]{2,1,0:T(8,128)(2,1)S(1)}, bf16[2,1024,512]{2,1,0:T(8,128)(2,1)S(1)}) fusion(f32[1024,512]{1,0:T(8,128)S(1)} %get-tuple-element.158, f32[2]{0:T(128)S(1)} %bitcast.94, f32[1024,512]{1,0:T(8,128)S(1)} %get-tuple-element.159), kind=kLoop, calls=%fused_computation.2.clone.1 | loop fusion | flops 6291456 | bytes 8388616 | tf_op jit(solution)/shard_map/while/body/eval_jaxpr/convert_element_type | solution.py:33
  143.0 0.4 convolution_bitcast_fusion.11
  144.3 0.7 dynamic-slice_bitcast_fusion.2
  145.0 0.9 multiply_reduce_fusion.3
  145.9 0.7 rsqrt_multiply_fusion.2
  146.6 16.1 %multiply_convert_fusion.5 = (bf16[2,1024,512]{2,1,0:T(8,128)(2,1)S(1)}, bf16[2,1024,512]{2,1,0:T(8,128)(2,1)S(1)}) fusion(f32[1024,512]{1,0:T(8,128)S(1)} %get-tuple-element.158, f32[2]{0:T(128)S(1)} %bitcast.94, f32[1024,512]{1,0:T(8,128)S(1)} %get-tuple-element.159), kind=kLoop, calls=%fused_computation.2.clone.1 | loop fusion | flops 6291456 | bytes 8388616 | tf_op jit(solution)/shard_map/while/body/eval_jaxpr/convert_element_type | solution.py:33
  163.1 0.4 convolution_bitcast_fusion.11
  164.4 0.7 dynamic-slice_bitcast_fusion.2
  165.1 0.9 multiply_reduce_fusion.3
  166.1 0.7 rsqrt_multiply_fusion.2
  166.8 16.1 %multiply_convert_fusion.5 = (bf16[2,1024,512]{2,1,0:T(8,128)(2,1)S(1)}, bf16[2,1024,512]{2,1,0:T(8,128)(2,1)S(1)}) fusion(f32[1024,512]{1,0:T(8,128)S(1)} %get-tuple-element.158, f32[2]{0:T(128)S(1)} %bitcast.94, f32[1024,512]{1,0:T(8,128)S(1)} %get-tuple-element.159), kind=kLoop, calls=%fused_computation.2.clone.1 | loop fusion | flops 6291456 | bytes 8388616 | tf_op jit(solution)/shard_map/while/body/eval_jaxpr/convert_element_type | solution.py:33
  183.3 0.4 convolution_bitcast_fusion.11
  184.5 0.7 dynamic-slice_bitcast_fusion.2
  185.3 0.9 multiply_reduce_fusion.3
  186.2 0.7 rsqrt_multiply_fusion.2
  186.9 16.1 %multiply_convert_fusion.5 = (bf16[2,1024,512]{2,1,0:T(8,128)(2,1)S(1)}, bf16[2,1024,512]{2,1,0:T(8,128)(2,1)S(1)}) fusion(f32[1024,512]{1,0:T(8,128)S(1)} %get-tuple-element.158, f32[2]{0:T(128)S(1)} %bitcast.94, f32[1024,512]{1,0:T(8,128)S(1)} %get-tuple-element.159), kind=kLoop, calls=%fused_computation.2.clone.1 | loop fusion | flops 6291456 | bytes 8388616 | tf_op jit(solution)/shard_map/while/body/eval_jaxpr/convert_element_type | solution.py:33
  204.7 0.7 dynamic-slice_bitcast_fusion.2
  205.4 0.9 multiply_reduce_fusion.3
  206.4 0.7 rsqrt_multiply_fusion.2
  207.0 16.1 %multiply_convert_fusion.5 = (bf16[2,1024,512]{2,1,0:T(8,128)(2,1)S(1)}, bf16[2,1024,512]{2,1,0:T(8,128)(2,1)S(1)}) fusion(f32[1024,512]{1,0:T(8,128)S(1)} %get-tuple-element.158, f32[2]{0:T(128)S(1)} %bitcast.94, f32[1024,512]{1,0:T(8,128)S(1)} %get-tuple-element.159), kind=kLoop, calls=%fused_computation.2.clone.1 | loop fusion | flops 6291456 | bytes 8388616 | tf_op jit(solution)/shard_map/while/body/eval_jaxpr/convert_element_type | solution.py:33
  224.9 0.8 squeeze_reshape.3
  225.7 88.8 %all-reduce.2.cloned.1.call-done = f32[2,2,8192]{2,1,0:T(2,128)} async-done(((f32[2,2,8192]{2,1,0:T(2,128)}), f32[2,2,8192]{2,1,0:T(2,128)}) %all-reduce.2.cloned.1.call-update) | async-done | bytes 131088 | tf_op jit(solution)/shard_map/psum | solution.py:83
  314.4 0.7 multiply_reduce_fusion.1
  315.2 134.6 %psum.15 = f32[1024]{0:T(1024)S(1)} all-reduce(f32[1024]{0:T(1024)S(1)} %multiply_reduce_fusion.1), channel_id=1, replica_groups=mesh['tm'=64,'mic'=8] {'tm'}, use_global_device_ids=true, to_apply=%region_5.6 | all-reduce | flops 1024 | bytes 8192 | tf_op jit(solution)/shard_map/psum | solution.py:86
  449.8 0.6 broadcast_multiply_fusion
  (69 shorter events, 11.3 us)
Async XLA Ops:
  6.5 307.9 %all-reduce.2.cloned.1.call-start = ((), (), s32[]{:S(2)}) async-start(), calls=%async_computation | async-start | bytes 262144 | tf_op jit(solution)/shard_map/psum | solution.py:83
  6.5 52.5 %collective-permute-start = (bf16[4096,512]{1,0:T(8,128)(2,1)}, bf16[4096,512]{1,0:T(8,128)(2,1)}, u32[]{:S(2)}, u32[]{:S(2)}) collective-permute-start(bf16[4096,512]{1,0:T(8,128)(2,1)} %param.6), channel_id=1, source_target_pairs={{8,0},{16,8},{24,16},{32,24},{40,32},{48,40},{56,48},{64,56},{72,6... | collective-permute-start | bytes 12582920 | tf_op jit(solution)/shard_map/ppermute | solution.py:15
  18.3 45.5 %copy-start = (s32[3,512]{1,0:T(4,128)S(1)}, s32[3,512]{1,0:T(4,128)}, u32[]{:S(2)}) copy-start(s32[3,512]{1,0:T(4,128)} %param.7) | copy-start | bytes 18436
Sparse Core Ops, SparseCore 0:
  225.8 88.5 all-reduce.1
where the time goes:
time: 458 us; the launch traced here: 457 us
  other arithmetic  147 us (32%)
  blocking collectives  135 us (29%)
  waiting for transfers between devices  130 us (28%)
  matrix products  16.7 us (4%)
  between operations  13.5 us (3%)
  starting transfers between devices  8.78 us (2%)
  local copies, waits for them, and re-layouts  6.75 us (1%)
    psum x1, blocking collectives, local(): power_sum = lax.psum(local_power, 'tm')  135 us
    convert_element_type x8, other arithmetic, steer_block(): (strength[None] * jnp.cos(2.0 * math.pi * cycles)).astype(jnp.bfloat16)  129 us
    psum x1, waiting for transfers between devices, local(): summed = lax.psum(partial_value, 'mic')  88.8 us
    ppermute x1, waiting for transfers between devices, from_behind(): return lax.ppermute(shard, axis, pairs)  40.8 us
  transfers between devices with their start and end apart: 2, of which 2 were waited for; matrix products, arithmetic and copies ran while one was open for 1% of the time, Pallas kernels for 0%

commit v1 on v0

--- a/solution.py
+++ b/solution.py
@@ -83,7 +83,8 @@
     summed = lax.psum(partial_value, "mic")
     owned = lax.dynamic_slice_in_dim(summed, lax.axis_index("mic") * owned_count, owned_count, 2)
     local_power = jnp.sum(owned * owned, axis=(0, 1))
-    power_sum = lax.psum(local_power, "tm")
+    _test_stacks_all = lambda w_in: lax.all_gather(w_in, axis_name="tm").sum(axis=0)
+    power_sum = _test_stacks_all(local_power)
     return power_sum / (spans * NBINS * MICS)
 
 

time: 458 us -> 407 us (0.89)
  blocking collectives: 135 us -> 83.5 us
    psum x1 -> x0, blocking collectives: 135 us -> none  [local(): power_sum = lax.psum(local_power, 'tm')]
    all_gather x0 -> x1, blocking collectives: none -> 83.5 us  [local(): lax.all_gather(w_in, axis_name='tm').sum(axis=0)]
where the time goes in v1:
time: 407 us; the launch traced here: 406 us
  other arithmetic  147 us (36%)
  waiting for transfers between devices  130 us (32%)
  blocking collectives  83.5 us (21%)
  matrix products  16.7 us (4%)
  between operations  13.5 us (3%)
  starting transfers between devices  8.78 us (2%)
  local copies, waits for them, and re-layouts  6.79 us (2%)
    convert_element_type x8, other arithmetic, steer_block(): (strength[None] * jnp.cos(2.0 * math.pi * cycles)).astype(jnp.bfloat16)  129 us
    psum x1, waiting for transfers between devices, local(): summed = lax.psum(partial_value, 'mic')  88.8 us
    all_gather x1, blocking collectives, local(): lax.all_gather(w_in, axis_name='tm').sum(axis=0)  83.5 us
    ppermute x1, waiting for transfers between devices, from_behind(): return lax.ppermute(shard, axis, pairs)  40.8 us
    ppermute x1, starting transfers between devices, from_behind(): return lax.ppermute(shard, axis, pairs)  8.78 us
  transfers between devices with their start and end apart: 2, of which 2 were waited for; matrix products, arithmetic and copies ran while one was open for 1% of the time, Pallas kernels for 0%

profile of v1, /device:TPU:1, one launch (start us, length us, event | category | flops | bytes accessed | tf_op | source)
XLA Modules:
  0.0 406.2 jit_solution(14925376594284844673)
XLA Ops:
  6.5 8.8 %collective-permute-start = (bf16[4096,512]{1,0:T(8,128)(2,1)}, bf16[4096,512]{1,0:T(8,128)(2,1)}, u32[]{:S(2)}, u32[]{:S(2)}) collective-permute-start(bf16[4096,512]{1,0:T(8,128)(2,1)} %param.6), channel_id=1, source_target_pairs={{8,0},{16,8},{24,16},{32,24},{40,32},{48,40},{56,48},{64,56},{72,6... | collective-permute-start | bytes 12582920 | tf_op jit(solution)/shard_map/ppermute | solution.py:15
  15.5 1.9 multiply_convert_fusion.3
  17.6 0.7 convert_bitcast_fusion
  18.3 40.8 %collective-permute-done = bf16[4096,512]{1,0:T(8,128)(2,1)} collective-permute-done((bf16[4096,512]{1,0:T(8,128)(2,1)}, bf16[4096,512]{1,0:T(8,128)(2,1)}, u32[]{:S(2)}, u32[]{:S(2)}) %collective-permute-start) | collective-permute-done | bytes 4194336 | tf_op jit(solution)/shard_map/ppermute | solution.py:15
  59.1 4.6 %fusion.16 = bf16[1,4,512]{2,1,0:T(4,128)(2,1)S(1)} fusion(bf16[4,8192]{1,0:T(4,128)(2,1)S(1)} %convert_element_type.74, bf16[4096,512]{1,0:T(8,128)(2,1)} %collective-permute-done, bf16[4096,512]{1,0:T(8,128)(2,1)} %param.6), kind=kOutput, calls=%fused_computation.36 | convolution fusion | flops 50333696 | bytes 8458240 | tf_op jit(solution)/shard_map/dot_general | solution.py:76
  63.7 161.1 %while.12 = (s32[]{:T(128)}, f32[8,1,2,2,1024]{4,3,2,1,0:T(2,128)S(1)}, s32[8,3,1024]{2,1,0:T(4,128)}, s32[3,512]{1,0:T(4,128)S(1)}, f32[2,1,1]{0,2,1:T(1,128)S(1)}, /*index=5*/bf16[1,4,512]{2,1,0:T(4,128)(2,1)S(1)}, s32[]{:T(128)}) while((s32[]{:T(128)}, f32[8,1,2,2,1024]{4,3,2,1,0:T(2,128)S(1)}, s32[8,3,1024]{2,1,0:T(4,128)}, ...), condition=%wide.region_2.3_spmd, body=%wide.region_0.2_spmd.sunk | while | flops 19935232 | bytes 21170268 | solution.py:67
  63.7 0.7 dynamic-slice_bitcast_fusion.2
  64.5 0.9 multiply_reduce_fusion.3
  65.4 0.7 rsqrt_multiply_fusion.2
  66.1 16.1 %multiply_convert_fusion.5 = (bf16[2,1024,512]{2,1,0:T(8,128)(2,1)S(1)}, bf16[2,1024,512]{2,1,0:T(8,128)(2,1)S(1)}) fusion(f32[1024,512]{1,0:T(8,128)S(1)} %get-tuple-element.158, f32[2]{0:T(128)S(1)} %bitcast.94, f32[1024,512]{1,0:T(8,128)S(1)} %get-tuple-element.159), kind=kLoop, calls=%fused_computation.2.clone.1 | loop fusion | flops 6291456 | bytes 8388616 | tf_op jit(solution)/shard_map/while/body/eval_jaxpr/convert_element_type | solution.py:33
  83.9 0.7 dynamic-slice_bitcast_fusion.2
  84.6 0.9 multiply_reduce_fusion.3
  85.5 0.7 rsqrt_multiply_fusion.2
  86.2 16.1 %multiply_convert_fusion.5 = (bf16[2,1024,512]{2,1,0:T(8,128)(2,1)S(1)}, bf16[2,1024,512]{2,1,0:T(8,128)(2,1)S(1)}) fusion(f32[1024,512]{1,0:T(8,128)S(1)} %get-tuple-element.158, f32[2]{0:T(128)S(1)} %bitcast.94, f32[1024,512]{1,0:T(8,128)S(1)} %get-tuple-element.159), kind=kLoop, calls=%fused_computation.2.clone.1 | loop fusion | flops 6291456 | bytes 8388616 | tf_op jit(solution)/shard_map/while/body/eval_jaxpr/convert_element_type | solution.py:33
  102.7 0.4 convolution_bitcast_fusion.11
  104.0 0.7 dynamic-slice_bitcast_fusion.2
  104.7 0.9 multiply_reduce_fusion.3
  105.7 0.7 rsqrt_multiply_fusion.2
  106.4 16.1 %multiply_convert_fusion.5 = (bf16[2,1024,512]{2,1,0:T(8,128)(2,1)S(1)}, bf16[2,1024,512]{2,1,0:T(8,128)(2,1)S(1)}) fusion(f32[1024,512]{1,0:T(8,128)S(1)} %get-tuple-element.158, f32[2]{0:T(128)S(1)} %bitcast.94, f32[1024,512]{1,0:T(8,128)S(1)} %get-tuple-element.159), kind=kLoop, calls=%fused_computation.2.clone.1 | loop fusion | flops 6291456 | bytes 8388616 | tf_op jit(solution)/shard_map/while/body/eval_jaxpr/convert_element_type | solution.py:33
  122.9 0.4 convolution_bitcast_fusion.11
  124.1 0.7 dynamic-slice_bitcast_fusion.2
  124.9 0.9 multiply_reduce_fusion.3
  125.8 0.7 rsqrt_multiply_fusion.2
  126.5 16.1 %multiply_convert_fusion.5 = (bf16[2,1024,512]{2,1,0:T(8,128)(2,1)S(1)}, bf16[2,1024,512]{2,1,0:T(8,128)(2,1)S(1)}) fusion(f32[1024,512]{1,0:T(8,128)S(1)} %get-tuple-element.158, f32[2]{0:T(128)S(1)} %bitcast.94, f32[1024,512]{1,0:T(8,128)S(1)} %get-tuple-element.159), kind=kLoop, calls=%fused_computation.2.clone.1 | loop fusion | flops 6291456 | bytes 8388616 | tf_op jit(solution)/shard_map/while/body/eval_jaxpr/convert_element_type | solution.py:33
  143.0 0.4 convolution_bitcast_fusion.11
  144.3 0.7 dynamic-slice_bitcast_fusion.2
  145.0 0.9 multiply_reduce_fusion.3
  145.9 0.7 rsqrt_multiply_fusion.2
  146.6 16.1 %multiply_convert_fusion.5 = (bf16[2,1024,512]{2,1,0:T(8,128)(2,1)S(1)}, bf16[2,1024,512]{2,1,0:T(8,128)(2,1)S(1)}) fusion(f32[1024,512]{1,0:T(8,128)S(1)} %get-tuple-element.158, f32[2]{0:T(128)S(1)} %bitcast.94, f32[1024,512]{1,0:T(8,128)S(1)} %get-tuple-element.159), kind=kLoop, calls=%fused_computation.2.clone.1 | loop fusion | flops 6291456 | bytes 8388616 | tf_op jit(solution)/shard_map/while/body/eval_jaxpr/convert_element_type | solution.py:33
  163.1 0.4 convolution_bitcast_fusion.11
  164.4 0.7 dynamic-slice_bitcast_fusion.2
  165.1 0.9 multiply_reduce_fusion.3
  166.1 0.7 rsqrt_multiply_fusion.2
  166.8 16.1 %multiply_convert_fusion.5 = (bf16[2,1024,512]{2,1,0:T(8,128)(2,1)S(1)}, bf16[2,1024,512]{2,1,0:T(8,128)(2,1)S(1)}) fusion(f32[1024,512]{1,0:T(8,128)S(1)} %get-tuple-element.158, f32[2]{0:T(128)S(1)} %bitcast.94, f32[1024,512]{1,0:T(8,128)S(1)} %get-tuple-element.159), kind=kLoop, calls=%fused_computation.2.clone.1 | loop fusion | flops 6291456 | bytes 8388616 | tf_op jit(solution)/shard_map/while/body/eval_jaxpr/convert_element_type | solution.py:33
  183.3 0.4 convolution_bitcast_fusion.11
  184.5 0.7 dynamic-slice_bitcast_fusion.2
  185.3 0.9 multiply_reduce_fusion.3
  186.2 0.7 rsqrt_multiply_fusion.2
  186.9 16.1 %multiply_convert_fusion.5 = (bf16[2,1024,512]{2,1,0:T(8,128)(2,1)S(1)}, bf16[2,1024,512]{2,1,0:T(8,128)(2,1)S(1)}) fusion(f32[1024,512]{1,0:T(8,128)S(1)} %get-tuple-element.158, f32[2]{0:T(128)S(1)} %bitcast.94, f32[1024,512]{1,0:T(8,128)S(1)} %get-tuple-element.159), kind=kLoop, calls=%fused_computation.2.clone.1 | loop fusion | flops 6291456 | bytes 8388616 | tf_op jit(solution)/shard_map/while/body/eval_jaxpr/convert_element_type | solution.py:33
  204.7 0.7 dynamic-slice_bitcast_fusion.2
  205.4 0.9 multiply_reduce_fusion.3
  206.4 0.7 rsqrt_multiply_fusion.2
  207.0 16.1 %multiply_convert_fusion.5 = (bf16[2,1024,512]{2,1,0:T(8,128)(2,1)S(1)}, bf16[2,1024,512]{2,1,0:T(8,128)(2,1)S(1)}) fusion(f32[1024,512]{1,0:T(8,128)S(1)} %get-tuple-element.158, f32[2]{0:T(128)S(1)} %bitcast.94, f32[1024,512]{1,0:T(8,128)S(1)} %get-tuple-element.159), kind=kLoop, calls=%fused_computation.2.clone.1 | loop fusion | flops 6291456 | bytes 8388616 | tf_op jit(solution)/shard_map/while/body/eval_jaxpr/convert_element_type | solution.py:33
  224.9 0.8 squeeze_reshape.3
  225.7 88.8 %all-reduce.2.cloned.1.call-done = f32[2,2,8192]{2,1,0:T(2,128)} async-done(((f32[2,2,8192]{2,1,0:T(2,128)}), f32[2,2,8192]{2,1,0:T(2,128)}) %all-reduce.2.cloned.1.call-update) | async-done | bytes 131088 | tf_op jit(solution)/shard_map/psum | solution.py:83
  314.4 0.7 multiply_reduce_fusion.1
  315.2 83.5 %all-gather = f32[65536]{0:T(1024)S(1)} all-gather(f32[1024]{0:T(1024)S(1)} %multiply_reduce_fusion.1), channel_id=2, replica_groups=mesh['tm'=64,'mic'=8] {'tm'}, dimensions={0}, use_global_device_ids=true | all-gather | bytes 266240 | tf_op jit(solution)/shard_map/all_gather | solution.py:86
  398.8 0.6 broadcast_multiply_fusion
  (71 shorter events, 11.3 us)
Async XLA Ops:
  6.5 307.9 %all-reduce.2.cloned.1.call-start = ((), (), s32[]{:S(2)}) async-start(), calls=%async_computation | async-start | bytes 262144 | tf_op jit(solution)/shard_map/psum | solution.py:83
  6.5 52.5 %collective-permute-start = (bf16[4096,512]{1,0:T(8,128)(2,1)}, bf16[4096,512]{1,0:T(8,128)(2,1)}, u32[]{:S(2)}, u32[]{:S(2)}) collective-permute-start(bf16[4096,512]{1,0:T(8,128)(2,1)} %param.6), channel_id=1, source_target_pairs={{8,0},{16,8},{24,16},{32,24},{40,32},{48,40},{56,48},{64,56},{72,6... | collective-permute-start | bytes 12582920 | tf_op jit(solution)/shard_map/ppermute | solution.py:15
  18.3 45.5 %copy-start = (s32[3,512]{1,0:T(4,128)S(1)}, s32[3,512]{1,0:T(4,128)}, u32[]{:S(2)}) copy-start(s32[3,512]{1,0:T(4,128)} %param.7) | copy-start | bytes 18436
Sparse Core Ops, SparseCore 0:
  225.8 88.5 all-reduce.1
